TPU v7x, 256 devices: a whole 4x4x8 slice. The times are simulated.
256 devices in a mesh: rep: 16 (over z, y_hi), section: 4 (over y_lo, core), head: 4 (over x).
Axes of the slice: x: 4, y: 4 (y_hi: 2, y_lo: 2; y = y_hi * 2 + y_lo), z: 8, core: 2. Of those that a mesh axis runs over, the one named last changes fastest.
Arguments:
- prompt_pages: bfloat16 [16, 4, 16, 16, 2, 6144], P('rep', 'section', 'head'), may hold values from -6 to 6
- page_scales: bfloat16 [16, 4, 16, 2, 48], P('rep', 'section', 'head'), may hold values from 0.099609375 to 1.5
- page_table: int32 [16, 16], P('rep'), may hold values from 0 to 15, each once within a row
- lengths: int32 [16, 8], replicated, may hold values from 1 to 32, 160 in all within a row
- route: int32 [16, 8], replicated, may hold values from 0 to 15, as said below
- queries: bfloat16 [16, 4, 16, 2, 8, 6144], P('rep', None, None, None, None, ('section', 'head')), may hold values from -6 to 6
- new_kv: bfloat16 [16, 4, 16, 2, 8, 2, 6144], P('rep', None, None, None, None, None, ('section', 'head')), may hold values from -6 to 6
Outputs:
- decode_cache: bfloat16 [16, 4, 16, 2, 32, 2, 6144], P('rep', None, None, None, None, None, ('section', 'head'))
- decode_scales: bfloat16 [16, 4, 16, 2, 2, 2, 48], P('rep', None, None, None, None, None, ('section', 'head'))
- attention: bfloat16 [16, 4, 16, 2, 8, 6144], P('rep', None, None, None, None, ('section', 'head'))
Inputs may be any that keep to these rules, and one draw needn't show every extreme that they name: `page_table`: each row is a permutation of one instance's 16 page slots; page j of request q is entry q * 2 + j. `lengths`: each row sums to 160 and holds one length 32. `route`: no replica gets more than 2 requests of one instance, and in every draw one replica gets exactly 2 from every instance.
All inputs are finite; a program needn't handle non-finite values.
Results may differ from a plain program's by a relative error of at most 0.0049.
Values may be sent and summed in bfloat16 or wider, within the bound.
A program may use at most 128 MiB of HBM per device.

v0:
```python
import functools
import math

import jax
import jax.numpy as jnp
import numpy as np
from jax import lax
from jax.experimental import pallas as pl
from jax.experimental.pallas import tpu as pltpu
from jax.sharding import PartitionSpec as P

MESH = pl.DeviceIdType.MESH
NODES = 16
RING = NODES // 2
PORTS = 3
TIERS = (13, 14, 16)
ROUNDS = TIERS[-1]
PARTS = 4
REQS = 8
PAGE = 16
OFFSETS = (0, 0, 0, 0)

ROUTES = (
    0o5555555222222210, 0o5555555222222201, 0o4645121222121045, 0o5555212221210154,
    0o4612132222104545, 0o5531222222015554, 0o2212122210555646, 0o3121222101545455,
    0o1313121055555512, 0o2222210155555451, 0o1312105545565515, 0o2222015455555521,
    0o1310554545561212, 0o2201555555542221, 0o1055555555121212, 0o0155555454222222,
    0o5555552522222210, 0o5555552522222201, 0o5546222322221045, 0o5555522122220154,
    0o4526221222105645, 0o2122312131015554, 0o4323221310464555, 0o2232312101646565,
    0o2222231045454555, 0o3122220155646521, 0o2222105556454623, 0o3131015555542231,
    0o2210455656452312, 0o2101555564555232, 0o1045455546131312, 0o0154546565312122,
)


def links_of(source, dest, code):
    if code == 0:
        return []
    z, y = divmod(source, 2)
    step, mode = (1, (code - 1) % 3) if code <= 3 else (-1, (code - 1) % 3)
    cross = y != dest % 2
    hops = [2] if (cross and mode == 0) or (not cross and mode == 2) else []
    hops += [0 if step > 0 else 1] * (((dest // 2 - z) * step) % RING)
    if (cross and mode != 0) or (not cross and mode == 2):
        hops += [2]
    links = []
    for port in hops:
        links.append((z * 2 + y) * PORTS + port)
        if port == 2:
            y = 1 - y
        else:
            z = (z + (1 if port == 0 else -1)) % RING
    assert z * 2 + y == dest and len(links) < 8
    return links


def path_table():
    table = np.zeros((2, NODES, 8, NODES), np.float32)
    for rank in range(2):
        for source in range(NODES):
            for dest in range(NODES):
                code = (ROUTES[rank * NODES + source] >> (3 * dest)) & 7
                for hop, link in enumerate(links_of(source, dest, code)):
                    table[rank, dest, hop, source] = link + 1
    return table.reshape(2 * NODES * 8, NODES)


def plan_kernel(table_ref, inputs_ref, out_ref, sends, slots, spans):
    f32 = jnp.float32
    lane = lax.broadcasted_iota(jnp.int32, (1, 128), 1)
    source = lane // REQS
    order = lane % REQS
    pick = lax.broadcasted_iota(jnp.int32, (REQS, 128), 1) % REQS
    pick = pick == lax.broadcasted_iota(jnp.int32, (REQS, 128), 0)
    pick = jnp.where(pick, 1.0, 0.0).astype(jnp.bfloat16)

    def flat(ref):
        x = jnp.dot(ref.astype(jnp.bfloat16), pick, preferred_element_type=f32)
        x = jnp.where(node == source, x, 0.0)
        return jnp.sum(x, axis=0, keepdims=True)

    node = lax.broadcasted_iota(jnp.int32, (NODES, 128), 0)
    route = flat(inputs_ref[:NODES]).astype(jnp.int32)
    length = flat(inputs_ref[NODES:])
    rank = jnp.zeros_like(route)
    for back in range(1, REQS):
        earlier = pltpu.roll(route, back, axis=1)
        rank = rank + jnp.where((earlier == route) & (order >= back), 1, 0)
    count = jnp.sum(jnp.where(node == route, 1.0, 0.0), axis=1, keepdims=True)
    most = jnp.max(count, axis=0, keepdims=True)
    nodes = lax.broadcasted_iota(jnp.int32, (NODES, 1), 0).astype(f32)
    hot = jnp.min(jnp.where(count == most, nodes, 99.0), axis=0, keepdims=True).astype(jnp.int32)
    hot_z, hot_y = hot // 2, hot % 2

    def relative(x):
        y = x % 2
        return ((x // 2 - hot_z + RING) % RING) * 2 + (y + hot_y - 2 * y * hot_y)

    source_rel, dest_rel = relative(source), relative(route)
    from_one = jnp.where(node == source_rel, 1.0, 0.0).astype(jnp.bfloat16)
    every = jnp.dot(table_ref[...], from_one, preferred_element_type=f32)
    row = lax.broadcasted_iota(jnp.int32, (2 * NODES * 8, 128), 0) // 8
    every = jnp.where(row == rank * NODES + dest_rel, every, 0.0)
    path = every[0:8]
    for i in range(1, 2 * NODES):
        path = path + every[8 * i : 8 * i + 8]
    me = relative(jnp.zeros((1, 1), jnp.int32) + lax.axis_index("rep"))
    me_z, me_y = me // 2, me % 2
    up, down = (me_z + 1) % RING, (me_z + RING - 1) % RING
    to_me = (down * 2 + me_y, up * 2 + me_y, me_z * 2 + 1 - me_y)
    out_link = [(me * PORTS + k + 1).astype(f32) for k in range(PORTS)]
    in_link = [(to_me[k] * PORTS + k + 1).astype(f32) for k in range(PORTS)]
    link = lax.broadcasted_iota(jnp.int32, (NODES * PORTS, 128), 0).astype(f32) + 1.0
    tie = (127 - lane).astype(f32)
    hop_row = lax.broadcasted_iota(jnp.int32, (8, 128), 0)
    held = jnp.where(source_rel == me, order, 0).astype(f32)
    home = dest_rel == me
    own_slot = jnp.where(home, source * 2 + rank, 0).astype(f32)
    own_span = jnp.where(home, length, 0.0)
    for ref in (sends, slots, spans):
        ref[...] = jnp.zeros_like(ref)
    fine = []
    for t in range(ROUNDS):
        now = path[0:1]
        if t in TIERS:
            fine.append(jnp.max(now, axis=1, keepdims=True) == 0.0)
        left = jnp.sum(jnp.where(path > 0.0, 1.0, 0.0), axis=0, keepdims=True)
        key = left * 128.0 + tie
        asks = link == now
        first = jnp.max(jnp.where(asks, key, -1.0), axis=1, keepdims=True)
        wins = jnp.where(asks & (first == key), 1.0, 0.0)
        moves = jnp.max(wins, axis=0, keepdims=True) > 0.0
        for k in range(PORTS):
            leaves = moves & (now == out_link[k])
            sends[PORTS * t + k : PORTS * t + k + 1] = jnp.where(leaves, held, 0.0)
        for k in range(PORTS):
            comes = moves & (now == in_link[k])
            held = jnp.where(comes, float(REQS + PORTS * t + k), held)
            slots[PORTS * t + k : PORTS * t + k + 1] = jnp.where(comes, own_slot, 0.0)
            spans[PORTS * t + k : PORTS * t + k + 1] = jnp.where(comes, own_span, 0.0)
        later = jnp.where(hop_row < 7, pltpu.roll(path, 7, axis=0), 0.0)
        path = jnp.where(moves, later, path)
    fine.append(jnp.max(path[0:1], axis=1, keepdims=True) == 0.0)
    tier = sum(jnp.where(done, 0.0, 1.0) for done in fine)
    square = lax.broadcasted_iota(jnp.int32, (128, 128), 0) == lax.broadcasted_iota(
        jnp.int32, (128, 128), 1
    )

    def lay(rows):
        sums = jnp.sum(rows, axis=1, keepdims=True)
        n = rows.shape[0]
        return jnp.sum(jnp.where(square[:n], sums, 0.0), axis=0, keepdims=True)

    slot = lax.broadcasted_iota(jnp.int32, (2 * NODES, 128), 0)
    mine = (slot == source * 2 + rank) & home
    out = [
        lay(sends[...]),
        lay(jnp.where(mine, held, 0.0)),
        lay(jnp.where(mine, length, 0.0)),
        jnp.where(lane >= 0, tier, 0.0),
        lay(slots[...]),
        lay(spans[...]),
        jnp.zeros((2, 128), f32),
    ]
    out_ref[...] = jnp.concatenate(out, axis=0).astype(jnp.int32)


def plan(route, lengths):
    return pl.pallas_call(
        plan_kernel,
        out_shape=jax.ShapeDtypeStruct((8, 128), jnp.int32),
        in_specs=[pl.BlockSpec(memory_space=pltpu.VMEM)] * 2,
        out_specs=pl.BlockSpec(memory_space=pltpu.VMEM),
        scratch_shapes=[pltpu.VMEM((128, 128), jnp.float32)] * 3,
    )(jnp.asarray(path_table(), jnp.bfloat16), jnp.concatenate([route, lengths], axis=0))


def attend(known, new, queries, scale, span):
    f32 = jnp.float32
    bf16 = jnp.bfloat16
    layers = len(known)
    steps, feats = queries[0].shape
    heads = feats // 128
    rows = known[0].shape[0]
    total_rows = rows + new[0].shape[0]
    per_layer = heads * steps
    over = (((1,), (1,)), ((), ()))
    row = lax.broadcasted_iota(jnp.int32, (total_rows, 128), 0)
    lane = lax.broadcasted_iota(jnp.int32, (total_rows, 128), 1)
    even = row % 2 == 0
    part = rows // PARTS
    page = row % part // (part // 2)
    token = PAGE * page + row // part * (PAGE // PARTS) + row % (part // 2) // 2
    fresh = (row >= rows) & ((row - rows) // 2 <= lane % steps)
    valid = even & (((row < rows) & (token < span)) | fresh)
    own_head = lax.broadcasted_iota(jnp.int32, (128, 128), 0)
    own_head = own_head == lax.broadcasted_iota(jnp.int32, (128, 128), 1) // steps
    own_head = jnp.where(own_head, 1.0, 0.0).astype(bf16)
    block = lax.broadcasted_iota(jnp.int32, (per_layer, feats), 1) // 128
    block = block == lax.broadcasted_iota(jnp.int32, (per_layer, feats), 0) // steps

    both = [jnp.concatenate([known[l], new[l]], axis=0) for l in range(layers)]
    query = []
    for one in queries:
        one = jnp.concatenate([one.astype(f32)] * heads, axis=0)
        query.append(jnp.where(block, one, 0.0))
    query.append(jnp.zeros((128 - layers * per_layer, feats), f32))
    query = jnp.concatenate(query, axis=0).astype(bf16)
    score = lax.dot_general(both[0], query, over, preferred_element_type=f32)
    for l in range(1, layers):
        other = lax.dot_general(both[l], query, over, preferred_element_type=f32)
        score = jnp.where(lane // per_layer == l, other, score)
    scale = scale.astype(f32)
    scale = ((scale[0] + scale[1]) + (scale[2] + scale[3])).reshape(4, 128)
    scale = jnp.concatenate([scale, jnp.zeros((12, 128), f32)], axis=0).astype(bf16)
    scale = jnp.dot(scale, own_head, preferred_element_type=f32)
    factor = jnp.where(
        page == 0,
        jnp.where(even, scale[0:1], scale[1:2]),
        jnp.where(even, scale[2:3], scale[3:4]),
    )
    factor = jnp.where(row < rows, factor, 1.0)
    score = jnp.where(valid, score * factor / math.sqrt(128), -jnp.inf)
    power = jnp.exp(score - jnp.max(score, axis=0, keepdims=True))
    total = jnp.sum(power, axis=0, keepdims=True)
    weight = (pltpu.roll(power, 1, axis=0) * factor / total).T
    results = []
    for l in range(layers):
        own = weight[per_layer * l : per_layer * (l + 1)].astype(bf16)
        result = jnp.dot(own, both[l], preferred_element_type=f32)
        parts = [
            result[steps * h : steps * h + steps, 128 * h : 128 * h + 128] for h in range(heads)
        ]
        results.append(jnp.concatenate(parts, axis=1).astype(bf16))
    return results


def exchange_kernel(rounds, plan_ref, table_ref, pages, scales, query_hbm, new_hbm, *refs):
    streams = PARTS + 1
    stores = refs[:streams]
    att = refs[streams]
    refs = refs[streams + 1 :]
    groups = refs[:streams]
    lands = refs[streams : 2 * streams]
    packs = refs[2 * streams : 3 * streams]
    queries, news, group_send, group_recv, send_sem, recv_sem, new_sem = refs[3 * streams :]
    rep = lax.axis_index("rep")
    section = lax.axis_index("section")
    head = lax.axis_index("head")
    tokens = groups[0].shape[2]
    held = pages.shape[2]
    feats = groups[0].shape[4]
    layers, _, steps, _ = queries.shape

    peers = []
    for o in range(16):
        peers.append((lax.rem(section + o // 4, 4), lax.rem(head + o % 4, 4)))
    neighbours = (
        lax.rem(rep + 2, NODES),
        lax.rem(rep + NODES - 2, NODES),
        rep + 1 - 2 * lax.rem(rep, 2),
    )
    barrier = pltpu.get_barrier_semaphore()
    for s, h in peers[1:]:
        pl.semaphore_signal(barrier, inc=1, device_id=(rep, s, h), device_id_type=MESH)
    for n in neighbours:
        pl.semaphore_signal(barrier, inc=1, device_id=(n, section, head), device_id_type=MESH)
    pl.semaphore_wait(barrier, 15 + PORTS)

    def block(i, group):
        if i == PARTS:
            return scales.at[group]
        columns = pl.ds(pl.multiple_of(group * feats, 128), feats)
        return pages.at[0, 0, :, pl.ds(tokens * i, tokens), :, columns]

    def place(i, s, h):
        return groups[i].at[s, pl.ds(held * h, held)]

    def regroup(i, o):
        s, h = peers[o]
        return pltpu.make_async_remote_copy(
            src_ref=block(i, s * 4 + h),
            dst_ref=place(i, section, head),
            send_sem=group_send.at[i, o],
            recv_sem=group_recv.at[i, o],
            device_id=(rep, s, h),
            device_id_type=MESH,
        )

    def regroup_own(i):
        return pltpu.make_async_copy(
            block(i, section * 4 + head), place(i, section, head), group_recv.at[i, 0]
        )

    order = [PARTS] + list(range(PARTS))
    for i in order:
        for o in range(1, 16):
            regroup(i, o).start()
        regroup_own(i).start()
    load_query = pltpu.make_async_copy(query_hbm, queries, new_sem.at[0])
    load_new = pltpu.make_async_copy(new_hbm, news, new_sem.at[1])
    load_query.start()
    load_new.start()

    def send(i, slot, k):
        return pltpu.make_async_remote_copy(
            src_ref=packs[i].at[slot, k],
            dst_ref=lands[i].at[slot, k],
            send_sem=send_sem.at[i, slot, k],
            recv_sem=recv_sem.at[i, slot, k],
            device_id=(neighbours[k], section, head),
            device_id_type=MESH,
        )

    def compose(i, t, slot):
        for k in range(PORTS):
            packs[i][slot, k] = stores[i][plan_ref[0, PORTS * t + k]]
        for k in range(PORTS):
            send(i, slot, k).start()

    def arrive(i, t, slot):
        for k in range(PORTS):
            send(i, slot, k).wait_recv()
        for k in range(PORTS):
            stores[i][REQS + PORTS * t + k] = lands[i][slot, k]

    def attend_unit(at, unit, slot, span):
        known = [
            jnp.concatenate(
                [stores[i][unit, l].reshape(4 * tokens, feats) for i in range(PARTS)], axis=0
            )
            for l in range(layers)
        ]
        new = [news[l, slot].reshape(2 * steps, feats) for l in range(layers)]
        query = [queries[l, slot] for l in range(layers)]
        results = attend(known, new, query, stores[PARTS][unit], span)
        for l in range(layers):
            att[at, l] = results[l]

    def attend_own():
        for c in range(2):
            slot = 2 * rep + c
            attend_unit(c, plan_ref[1, slot], slot, plan_ref[2, slot])

    def attend_arrived(t):
        for k in range(PORTS):
            at = PORTS * t + k
            attend_unit(REQS + at, REQS + at, plan_ref[4, at], plan_ref[5, at])

    lag = OFFSETS + (0,)
    most = max(lag)

    def first(i):
        regroup_own(i).wait()
        for o in range(1, 16):
            regroup(i, o).wait_recv()
        for q in range(REQS):
            for j in range(2):
                stores[i][q, :, j] = groups[i][:, table_ref[0, 2 * q + j]]
        compose(i, 0, 0)

    def attend_at(time, k):
        if isinstance(time, int) and not 0 < time - most <= rounds:
            return
        at = PORTS * (time - most - 1) + k
        attend_unit(REQS + at, REQS + at, plan_ref[4, at], plan_ref[5, at])

    def beat(time):
        for n, i in enumerate(order):
            t = time - lag[i]
            if not isinstance(time, int):
                slot = lax.rem(t, 2)
                arrive(i, t - 1, 1 - slot)
                for k in range(PORTS):
                    send(i, slot, k).wait_send()
                compose(i, t, slot)
            elif t == 0:
                first(i)
            elif 0 < t <= rounds:
                arrive(i, t - 1, (t - 1) % 2)
                if t >= 2 and t < rounds:
                    for k in range(PORTS):
                        send(i, t % 2, k).wait_send()
                if t < rounds:
                    compose(i, t, t % 2)
            if n == PARTS:
                for k in range(PORTS):
                    attend_at(time, k)

    for time in range(most + 2):
        beat(time)
        if time == most:
            load_query.wait()
            load_new.wait()
            attend_own()

    def one(time, carry):
        beat(time)
        return carry

    lax.fori_loop(most + 2, rounds, one, 0)
    for time in range(rounds, rounds + most + 2):
        beat(time)
    for i in order:
        for slot in range(2):
            for k in range(PORTS):
                send(i, slot, k).wait_send()
        for o in range(1, 16):
            regroup(i, o).wait_send()


def exchange(rounds, steps, page_table, pages, scales, queries, new_kv):
    layers, nodes, cap, step_count, feats = queries.shape[1:]
    held = pages.shape[2]
    tokens = pages.shape[3] // PARTS
    store = REQS + PORTS * rounds
    units = [(tokens, 2, feats)] * PARTS + [(2, 128)]
    bf16 = jnp.bfloat16
    anywhere = pl.BlockSpec(memory_space=pl.ANY)
    smem = pl.BlockSpec(memory_space=pltpu.SMEM)
    vmem = pl.BlockSpec(memory_space=pltpu.VMEM)
    scratch = [pltpu.VMEM((layers, 4 * held) + u, bf16) for u in units]
    scratch += [pltpu.VMEM((2, PORTS, layers, 2) + u, bf16) for u in units] * 2
    query_shape = (layers, nodes * cap, step_count, feats)
    new_shape = (layers, nodes * cap, step_count, 2, feats)
    scratch += [pltpu.VMEM(query_shape, bf16), pltpu.VMEM(new_shape, bf16)]
    dma = pltpu.SemaphoreType.DMA
    streams = PARTS + 1
    scratch += [dma((streams, 16)), dma((streams, 16))]
    scratch += [dma((streams, 2, PORTS)), dma((streams, 2, PORTS)), dma((2,))]
    return pl.pallas_call(
        functools.partial(exchange_kernel, rounds),
        out_shape=[jax.ShapeDtypeStruct((store, layers, 2) + u, bf16) for u in units]
        + [jax.ShapeDtypeStruct((store, layers, step_count, feats), bf16)],
        in_specs=[smem, smem] + [anywhere] * 4,
        out_specs=[vmem] * (streams + 1),
        scratch_shapes=scratch,
        compiler_params=pltpu.CompilerParams(
            collective_id=rounds, has_side_effects=True, vmem_limit_bytes=40 << 20
        ),
        cost_estimate=pl.CostEstimate(flops=0, bytes_accessed=20 << 20, transcendentals=0),
    )(
        steps,
        page_table,
        pages,
        scales,
        queries.reshape(query_shape),
        new_kv.reshape(new_shape),
    )


def place_kernel(plan_ref, *refs):
    units, scales, att = refs[:PARTS], refs[PARTS], refs[PARTS + 1]
    cache_hbm, scales_ref, att_hbm, zero_unit, zero_att, sems = refs[PARTS + 2 :]
    layers, slots, _, _, heads = scales_ref.shape
    tokens = units[0].shape[3]
    cap = 2
    rep = lax.axis_index("rep")
    zero_unit[...] = jnp.zeros_like(zero_unit)
    zero_att[...] = jnp.zeros_like(zero_att)

    def copies(i, live):
        unit = plan_ref[1, i]
        at = jnp.where(i // cap == rep, i % cap, unit)
        out = []
        for s in range(PARTS):
            to = cache_hbm.at[0, :, i // cap, i % cap, :, pl.ds(tokens * s, tokens)]
            source = units[s].at[unit] if live else zero_unit
            out.append(pltpu.make_async_copy(source, to, sems.at[i, s]))
        source = att.at[at] if live else zero_att
        to = att_hbm.at[0, :, i // cap, i % cap]
        return out + [pltpu.make_async_copy(source, to, sems.at[i, PARTS])]

    @pl.loop(0, slots)
    def _(i):
        @pl.when(plan_ref[2, i] > 0)
        def _():
            for copy in copies(i, True):
                copy.start()
            scale = scales[plan_ref[1, i]]
            for l in range(layers):
                scales_ref[l, i] = scale[l][:, :, heads * l : heads * l + heads]

        @pl.when(plan_ref[2, i] == 0)
        def _():
            for copy in copies(i, False):
                copy.start()
            for l in range(layers):
                scales_ref[l, i] = jnp.zeros((2, 2, heads), scales_ref.dtype)

    @pl.loop(0, slots)
    def _(i):
        for copy in copies(i, False):
            copy.wait()


def place(steps, units, queries):
    layers, nodes, cap, step_count, feats = queries.shape[1:]
    heads = feats // 128
    bf16 = jnp.bfloat16
    anywhere = pl.BlockSpec(memory_space=pl.ANY)
    vmem = pl.BlockSpec(memory_space=pltpu.VMEM)
    smem = pl.BlockSpec(memory_space=pltpu.SMEM)
    cache, scales, attention = pl.pallas_call(
        place_kernel,
        in_specs=[smem] + [vmem] * len(units),
        out_specs=[anywhere, vmem, anywhere],
        out_shape=[
            jax.ShapeDtypeStruct((1, layers, nodes, cap, 2, PAGE, 2, feats), bf16),
            jax.ShapeDtypeStruct((layers, nodes * cap, 2, 2, heads), bf16),
            jax.ShapeDtypeStruct(queries.shape, bf16),
        ],
        scratch_shapes=[
            pltpu.VMEM(units[0].shape[1:], bf16),
            pltpu.VMEM(units[PARTS + 1].shape[1:], bf16),
            pltpu.SemaphoreType.DMA((nodes * cap, PARTS + 1)),
        ],
        compiler_params=pltpu.CompilerParams(vmem_limit_bytes=40 << 20),
    )(steps, *units)
    cache = cache.reshape(1, layers, nodes, cap, 2 * PAGE, 2, feats)
    return cache, scales.reshape(1, layers, nodes, cap, 2, 2, heads), attention


def slot_ranks(route):
    req_ids = jnp.arange(route.shape[1], dtype=jnp.int32)
    same_dest = route[:, :, None] == route[:, None, :]
    earlier = req_ids[None, :] < req_ids[:, None]
    return jnp.sum((same_dest & earlier[None]).astype(jnp.int32), axis=2)


def padded(prompt_pages, page_scales, page_table, lengths, route, queries, new_kv):
    rep_count = lax.axis_size("rep")
    section_count = lax.axis_size("section")
    head_count = lax.axis_size("head")
    replica = lax.axis_index("rep")
    layers_here = prompt_pages.shape[1]
    pages_here = prompt_pages.shape[2]
    page_rows = prompt_pages.shape[3]
    feature_count = prompt_pages.shape[5]
    heads_total = page_scales.shape[4]
    head_dim = feature_count // heads_total
    group_count = section_count * head_count
    feat_here = feature_count // group_count
    heads_here = heads_total // group_count
    req_count = route.shape[1]
    capacity = max(2, req_count // rep_count)
    pages_each = page_table.shape[1] // req_count
    layer_count = layers_here * section_count
    span_max = page_rows * pages_each
    steps_count = queries.shape[4]
    req_ids = jnp.arange(req_count, dtype=jnp.int32)
    dest_ids = jnp.arange(rep_count, dtype=jnp.int32)
    cap_ids = jnp.arange(capacity, dtype=jnp.int32)
    page_ids = jnp.arange(pages_each, dtype=jnp.int32)
    slot_rank = slot_ranks(route)
    own_route = lax.dynamic_index_in_dim(route, replica, 0, keepdims=False)
    own_rank = lax.dynamic_index_in_dim(slot_rank, replica, 0, keepdims=False)
    send_match = (own_route[None, None, :] == dest_ids[:, None, None]) & (
        own_rank[None, None, :] == cap_ids[None, :, None]
    )
    send_live = jnp.any(send_match, axis=2)
    send_request = jnp.sum(jnp.where(send_match, req_ids[None, None, :], 0), axis=2)
    physical = page_table[0][send_request[:, :, None] * pages_each + page_ids[None, None, :]]
    recv_match = (route[:, None, :] == replica) & (slot_rank[:, None, :] == cap_ids[None, :, None])
    recv_live = jnp.any(recv_match, axis=2)
    slot_span = jnp.sum(jnp.where(recv_match, lengths[:, None, :], 0), axis=2)
    page_view = prompt_pages[0].reshape(
        layers_here, pages_here, page_rows, 2, section_count, head_count, feat_here
    )
    scale_view = page_scales[0].reshape(
        layers_here, pages_here, 1, 2, section_count, head_count, heads_here
    )
    zero_page = jnp.zeros((), prompt_pages.dtype)
    zero_scale = jnp.zeros((), page_scales.dtype)
    regrouped = (
        lax.all_to_all(
            lax.all_to_all(page_view, "section", split_axis=4, concat_axis=0, tiled=True),
            "head",
            split_axis=5,
            concat_axis=1,
            tiled=True,
        ),
        lax.all_to_all(
            lax.all_to_all(scale_view, "section", split_axis=4, concat_axis=0, tiled=True),
            "head",
            split_axis=5,
            concat_axis=1,
            tiled=True,
        ),
    )
    all_pages = regrouped[0].reshape(layer_count, pages_here * head_count, page_rows, 2, feat_here)
    all_scales = regrouped[1].reshape(layer_count, pages_here * head_count, 1, 2, heads_here)
    live_mask = send_live[None, :, :, None, None, None, None]
    slot_pages = jnp.where(live_mask, all_pages[:, physical], zero_page)
    slot_scales = jnp.where(live_mask, all_scales[:, physical], zero_scale)
    received = (
        lax.all_to_all(slot_pages, "rep", split_axis=1, concat_axis=1, tiled=True),
        lax.all_to_all(slot_scales, "rep", split_axis=1, concat_axis=1, tiled=True),
    )
    page_cache = received[0].reshape(layer_count, rep_count, capacity, span_max, 2, feat_here)
    scale_cache = received[1].reshape(layer_count, rep_count, capacity, pages_each, 2, heads_here)
    prompt_keys = page_cache[:, :, :, :, 0, :].reshape(
        layer_count, rep_count, capacity, span_max, heads_here, head_dim
    )
    prompt_values = page_cache[:, :, :, :, 1, :].reshape(
        layer_count, rep_count, capacity, span_max, heads_here, head_dim
    )
    query_rows = queries[0].reshape(
        layer_count, rep_count, capacity, steps_count, heads_here, head_dim
    )
    new_keys = new_kv[0][:, :, :, :, 0, :].reshape(
        layer_count, rep_count, capacity, steps_count, heads_here, head_dim
    )
    new_values = new_kv[0][:, :, :, :, 1, :].reshape(
        layer_count, rep_count, capacity, steps_count, heads_here, head_dim
    )
    score_root = math.sqrt(head_dim)
    key_scale = jnp.transpose(scale_cache[:, :, :, :, 0, :], (0, 1, 2, 4, 3))
    value_scale = jnp.transpose(scale_cache[:, :, :, :, 1, :], (0, 1, 2, 4, 3))
    prompt_dots = jnp.einsum(
        "lrcthd,lrckhd->lrchtk", query_rows, prompt_keys, preferred_element_type=jnp.float32
    )
    prompt_dots = prompt_dots.reshape(
        layer_count, rep_count, capacity, heads_here, steps_count, pages_each, page_rows
    )
    prompt_score = (
        prompt_dots * key_scale[:, :, :, :, None, :, None].astype(jnp.float32) / score_root
    )
    prompt_score = prompt_score.reshape(
        layer_count, rep_count, capacity, heads_here, steps_count, span_max
    )
    fresh_score = (
        jnp.einsum(
            "lrcthd,lrcuhd->lrchtu", query_rows, new_keys, preferred_element_type=jnp.float32
        )
        / score_root
    )
    visible = (jnp.arange(span_max, dtype=jnp.int32)[None, None, :] < slot_span[:, :, None])[
        None, :, :, None, None, :
    ]
    causal = (
        jnp.arange(steps_count, dtype=jnp.int32)[None, :]
        <= jnp.arange(steps_count, dtype=jnp.int32)[:, None]
    )
    row_max = jnp.maximum(
        jnp.max(jnp.where(visible, prompt_score, -jnp.inf), axis=-1, keepdims=True),
        jnp.max(jnp.where(causal, fresh_score, -jnp.inf), axis=-1, keepdims=True),
    )
    exp_prompt = jnp.where(visible, jnp.exp(prompt_score - row_max), 0.0)
    exp_fresh = jnp.where(causal, jnp.exp(fresh_score - row_max), 0.0)
    row_total = jnp.sum(exp_prompt, axis=-1, keepdims=True) + jnp.sum(
        exp_fresh, axis=-1, keepdims=True
    )
    value_weight = jnp.broadcast_to(
        value_scale[:, :, :, :, :, None], value_scale.shape + (page_rows,)
    )
    value_weight = value_weight.reshape(layer_count, rep_count, capacity, heads_here, span_max)[
        :, :, :, :, None, :
    ]
    prompt_weight = (exp_prompt * value_weight.astype(jnp.float32) / row_total).astype(jnp.bfloat16)
    fresh_weight = (exp_fresh / row_total).astype(jnp.bfloat16)
    attended = jnp.einsum(
        "lrchtk,lrckhd->lrcthd", prompt_weight, prompt_values, preferred_element_type=jnp.float32
    )
    attended = attended + jnp.einsum(
        "lrchtu,lrcuhd->lrcthd", fresh_weight, new_values, preferred_element_type=jnp.float32
    )
    attended = jnp.where(recv_live[None, :, :, None, None, None], attended, 0.0).astype(
        jnp.bfloat16
    )
    return (
        page_cache.reshape(1, layer_count, rep_count, capacity, span_max, 2, feat_here),
        scale_cache.reshape(1, layer_count, rep_count, capacity, pages_each, 2, heads_here),
        attended.reshape(1, layer_count, rep_count, capacity, steps_count, feat_here),
    )


def body(prompt_pages, page_scales, page_table, lengths, route, queries, new_kv):
    steps = plan(route, lengths)

    def direct(rounds, prompt_pages, page_scales, page_table, lengths, route, queries, new_kv):
        held = page_scales.shape[2]
        scales = page_scales.reshape(held, 2, 16, -1).transpose(2, 0, 1, 3)
        heads = scales.shape[3]
        scales = jnp.pad(jnp.tile(scales, (1, 1, 1, 4)), ((0, 0),) * 3 + ((0, 128 - 4 * heads),))
        own = jnp.arange(128) // heads == lax.axis_index("section")
        scales = jnp.where(own, scales, jnp.zeros((), scales.dtype))
        units = exchange(rounds, steps, page_table, prompt_pages, scales, queries, new_kv)
        return tuple(place(steps, units, queries))

    return lax.switch(
        len(TIERS) - steps[3, 0],
        [padded] + [functools.partial(direct, rounds) for rounds in TIERS[::-1]],
        prompt_pages,
        page_scales,
        page_table,
        lengths,
        route,
        queries,
        new_kv,
    )


def solution(mesh):
    return jax.shard_map(
        body,
        mesh=mesh,
        in_specs=(
            P("rep", "section", "head", None, None, None),
            P("rep", "section", "head", None, None),
            P("rep", None),
            P(),
            P(),
            P("rep", None, None, None, None, ("section", "head")),
            P("rep", None, None, None, None, None, ("section", "head")),
        ),
        out_specs=(
            P("rep", None, None, None, None, None, ("section", "head")),
            P("rep", None, None, None, None, None, ("section", "head")),
            P("rep", None, None, None, None, ("section", "head")),
        ),
        check_vma=False,
    )
```

profile of v0, /device:TPU:2, one launch (start us, length us, event | category | flops | bytes accessed | tf_op | source)
XLA Modules:
  0.0 104.8 jit_solution(12035157653924410628)
XLA Ops:
  0.6 0.8 pad_add_fusion
  1.4 0.7 copy.195.inputs_ref
  2.1 3.0 %shard_map.115 = s32[8,128]{1,0:T(8,128)S(1)} custom-call(bf16[256,16]{1,0:T(8,128)(2,1)} %constant.96.clone.table_ref, s32[32,8]{1,0:T(8,128)} %copy.195.inputs_ref), custom_call_target="tpu_custom_call" | custom-call | tf_op jit(solution)/shard_map/pallas_call | solution.py:168
  5.1 0.5 slice.21
  6.2 97.7 %conditional.1 = (bf16[1,4,16,2,32,2,384]{6,5,4,3,2,1,0:T(2,128)(2,1)}, bf16[1,4,16,2,8,384]{5,4,3,2,1,0:T(8,128)(2,1)S(1)}, bf16[1,4,16,2,2,2,3]{2,5,6,4,3,1,0:T(2,128)(2,1)S(1)}) conditional(s32[]{:T(128)} %bitcast.53, (s32[16,8]{0,1:T(8,128)}, bf16[1,1,4,16,2,6144]{5,4,3,2,1,0:T(2,128)(2,1)}, s32[1,16]{1,0:T(1,128)}, ...), branch_computations={%region_0.10_spmd, %region_10.11_spmd, %region_11.12_spmd, %region... | conditional | flops 68673144 | bytes 168208768 | solution.py:690
  6.7 0.8 reshape.234
  7.5 0.1 copy.166
  7.7 0.1 copy.167
  7.9 90.8 %branch_3_fun.2 = (bf16[47,4,2,4,2,384]{5,4,3,2,1,0:T(2,128)(2,1)S(1)}, bf16[47,4,2,4,2,384]{5,4,3,2,1,0:T(2,128)(2,1)S(1)}, bf16[47,4,2,4,2,384]{5,4,3,2,1,0:T(...) custom-call(s32[8,128]{1,0:T(8,128)S(1)} %get-tuple-element.87.plan_, ...), custom_call_target="tpu_custom_call" | custom-call | bytes 20971520 | tf_op jit(solution)/shard_map/cond/branch_3_fun/pallas_call | solution.py:430
  98.7 4.7 %branch_3_fun.3 = (bf16[1,4,16,2,2,16,2,384]{7,6,5,4,3,2,1,0:T(2,128)(2,1)}, bf16[4,32,2,2,3]{4,3,2,1,0:T(2,128)(2,1)S(1)}, bf16[1,4,16,2,8,384]{5,4,3,2,1,0:T(8,128)(2,1)S(1)}) custom-call(s32[8,128]{1,0:T(8,128)S(1)} %get-tuple-element.87.plan_ref, bf16[47,4,2,4,2,384]{5,4,3,2,1,0:T(2,128)(2,1)S(1)} %get-tuple-element.93.refs_0_, ...), custom_call_target="tpu_custom_call" | custom-call | tf_op jit(solution)/shard_map/cond/branch_3_fun/pallas_call | solution.py:503
  103.3 0.3 copy.207
  103.9 0.0 copy-start.9
  103.9 0.0 copy-start.11
  103.9 0.6 copy-done.9
  104.5 0.3 copy-done.11
  (3 shorter events, 0.1 us)
Async XLA Ops:
  103.9 0.6 copy-start.9
  103.9 0.9 copy-start.11
where the time goes:
time: 105 us
  Pallas kernels  98.4 us (94%)
  local copies, waits for them, and re-layouts  3.39 us (3%)
  between operations  1.32 us (1%)
    pallas_call x1, Pallas kernels, exchange(): pl.pallas_call(functools.partial(exchange_kernel, rounds), out_shape=[jax...  90.8 us
    pallas_call x1, Pallas kernels, place(): pl.pallas_call(place_kernel, in_specs=[smem] + [vmem] * len(units), out_s...  4.65 us
    pallas_call x1, Pallas kernels, plan(): pl.pallas_call(plan_kernel, out_shape=jax.ShapeDtypeStruct((8, 128), jnp....  2.96 us

commit v1 on v0

--- a/solution.py
+++ b/solution.py
@@ -13,7 +13,7 @@
 NODES = 16
 RING = NODES // 2
 PORTS = 3
-TIERS = (13, 14, 16)
+TIERS = (12, 13, 16)
 ROUNDS = TIERS[-1]
 PARTS = 4
 REQS = 8
@@ -21,15 +21,24 @@
 OFFSETS = (0, 0, 0, 0)
 
 ROUTES = (
-    0o5555555222222210, 0o5555555222222201, 0o4645121222121045, 0o5555212221210154,
-    0o4612132222104545, 0o5531222222015554, 0o2212122210555646, 0o3121222101545455,
-    0o1313121055555512, 0o2222210155555451, 0o1312105545565515, 0o2222015455555521,
-    0o1310554545561212, 0o2201555555542221, 0o1055555555121212, 0o0155555454222222,
-    0o5555552522222210, 0o5555552522222201, 0o5546222322221045, 0o5555522122220154,
-    0o4526221222105645, 0o2122312131015554, 0o4323221310464555, 0o2232312101646565,
-    0o2222231045454555, 0o3122220155646521, 0o2222105556454623, 0o3131015555542231,
-    0o2210455656452312, 0o2101555564555232, 0o1045455546131312, 0o0154546565312122,
+    0o5555555222222210, 0o5555555222222201, 0o4642121222221045, 0o5555212221210154,
+    0o4612132222104545, 0o5531222222015554, 0o2212122210555646, 0o3121222101655455,
+    0o1313221055555512, 0o2222220155555451, 0o1312105546565515, 0o2222015455555521,
+    0o1310554545561212, 0o2201555555542221, 0o1055555555151212, 0o0155555454222222,
+    0o5555461213122210, 0o5565652131222201, 0o5646262313221045, 0o5464522132320164,
+    0o2523221322105645, 0o2152312131015454, 0o1323231310464515, 0o2232313201546565,
+    0o2222131046565645, 0o3121210154656521, 0o2213104555454323, 0o2132015565655431,
+    0o2210465656454322, 0o3101646564653432, 0o1056565556422322, 0o0165646522223232,
+    0o5555555523222210, 0o5555553522222201, 0o4642122222221045, 0o5555322221220154,
+    0o4612122222104545, 0o5521222222015554, 0o1212222210554546, 0o2222222201545455,
+    0o1223121045555642, 0o2222320155546451, 0o1312105655455512, 0o2222015565555521,
+    0o1310454555551212, 0o2201545555552221, 0o1055555555121313, 0o0155555455222222,
+    0o5555461312222210, 0o6555655222322201, 0o4526221212221045, 0o6421213222220164,
+    0o1223222213105655, 0o2432212132016564, 0o4323231210465622, 0o3531312101656524,
+    0o2312231056464655, 0o3231210155655525, 0o1223104646561325, 0o3132015555656431,
+    0o1210555646465522, 0o2101655465242532, 0o1056455646252222, 0o0154556522552232,
 )
+TABLES = 4
 
 
 def links_of(source, dest, code):
@@ -54,14 +63,18 @@
 
 
 def path_table():
-    table = np.zeros((2, NODES, 8, NODES), np.float32)
-    for rank in range(2):
-        for source in range(NODES):
-            for dest in range(NODES):
-                code = (ROUTES[rank * NODES + source] >> (3 * dest)) & 7
-                for hop, link in enumerate(links_of(source, dest, code)):
-                    table[rank, dest, hop, source] = link + 1
-    return table.reshape(2 * NODES * 8, NODES)
+    table = np.zeros((TABLES, 2, NODES, 8, NODES), np.float32)
+    for n, rank in np.ndindex(TABLES, 2):
+        for source, dest in np.ndindex(NODES, NODES):
+            row, digit = source, dest
+            if n % 2:
+                row, digit = ((RING - x // 2) % RING * 2 + x % 2 for x in (source, dest))
+            code = (ROUTES[n // 2 * 32 + rank * NODES + row] >> (3 * digit)) & 7
+            if n % 2 and code:
+                code = (code + 2) % 6 + 1
+            for hop, link in enumerate(links_of(source, dest, code)):
+                table[n, rank, dest, hop, source] = link + 1
+    return table.reshape(TABLES * 2 * NODES * 8, NODES)
 
 
 def plan_kernel(table_ref, inputs_ref, out_ref, sends, slots, spans):
@@ -97,19 +110,33 @@
 
     source_rel, dest_rel = relative(source), relative(route)
     from_one = jnp.where(node == source_rel, 1.0, 0.0).astype(jnp.bfloat16)
-    every = jnp.dot(table_ref[...], from_one, preferred_element_type=f32)
-    row = lax.broadcasted_iota(jnp.int32, (2 * NODES * 8, 128), 0) // 8
-    every = jnp.where(row == rank * NODES + dest_rel, every, 0.0)
-    path = every[0:8]
-    for i in range(1, 2 * NODES):
-        path = path + every[8 * i : 8 * i + 8]
+    link = lax.broadcasted_iota(jnp.int32, (NODES * PORTS, 128), 0).astype(f32) + 1.0
+    length_of_table = 2 * NODES * 8
+    row = lax.broadcasted_iota(jnp.int32, (length_of_table, 128), 0) // 8
+    wanted = row == rank * NODES + dest_rel
+    path = fullest = None
+    for n in range(TABLES):
+        rows = table_ref[length_of_table * n : length_of_table * (n + 1)]
+        every = jnp.dot(rows, from_one, preferred_element_type=f32)
+        every = jnp.where(wanted, every, 0.0)
+        other = every[0:8]
+        for i in range(1, 2 * NODES):
+            other = other + every[8 * i : 8 * i + 8]
+        uses = jnp.where(link == other[0:1], 1.0, 0.0)
+        for hop in range(1, 7):
+            uses = uses + jnp.where(link == other[hop : hop + 1], 1.0, 0.0)
+        load = jnp.max(jnp.sum(uses, axis=1, keepdims=True), axis=0, keepdims=True)
+        if n == 0:
+            path, fullest = other, load
+        else:
+            path = jnp.where(load < fullest, other, path)
+            fullest = jnp.minimum(load, fullest)
     me = relative(jnp.zeros((1, 1), jnp.int32) + lax.axis_index("rep"))
     me_z, me_y = me // 2, me % 2
     up, down = (me_z + 1) % RING, (me_z + RING - 1) % RING
     to_me = (down * 2 + me_y, up * 2 + me_y, me_z * 2 + 1 - me_y)
     out_link = [(me * PORTS + k + 1).astype(f32) for k in range(PORTS)]
     in_link = [(to_me[k] * PORTS + k + 1).astype(f32) for k in range(PORTS)]
-    link = lax.broadcasted_iota(jnp.int32, (NODES * PORTS, 128), 0).astype(f32) + 1.0
     tie = (127 - lane).astype(f32)
     hop_row = lax.broadcasted_iota(jnp.int32, (8, 128), 0)
     held = jnp.where(source_rel == me, order, 0).astype(f32)

time: 105 us -> 103 us (0.981); the launches traced: 105 us -> 105 us
  no operation moved by 1% of the time
where the time goes in v1:
time: 103 us; the launch traced here: 105 us
  Pallas kernels  98.7 us (96%)
  local copies, waits for them, and re-layouts  3.39 us (3%)
  between operations  1.32 us (1%)
    pallas_call x1, Pallas kernels, exchange(): pl.pallas_call(functools.partial(exchange_kernel, rounds), out_shape=[jax...  90.8 us
    pallas_call x1, Pallas kernels, place(): pl.pallas_call(place_kernel, in_specs=[smem] + [vmem] * len(units), out_s...  4.68 us
    pallas_call x1, Pallas kernels, plan(): pl.pallas_call(plan_kernel, out_shape=jax.ShapeDtypeStruct((8, 128), jnp....  3.3 us

profile of v1, /device:TPU:2, one launch (start us, length us, event | category | flops | bytes accessed | tf_op | source)
XLA Modules:
  0.0 105.1 jit_solution(14360982672493078599)
XLA Ops:
  0.6 0.8 pad_add_fusion
  1.4 0.7 copy.195.inputs_ref
  2.1 3.3 %shard_map.115 = s32[8,128]{1,0:T(8,128)S(1)} custom-call(bf16[1024,16]{1,0:T(8,128)(2,1)} %constant.96.clone.table_ref, s32[32,8]{1,0:T(8,128)} %copy.195.inputs_ref), custom_call_target="tpu_custom_call" | custom-call | tf_op jit(solution)/shard_map/pallas_call | solution.py:195
  5.4 0.5 slice.21
  6.6 97.7 %conditional.1 = (bf16[1,4,16,2,32,2,384]{6,5,4,3,2,1,0:T(2,128)(2,1)}, bf16[1,4,16,2,8,384]{5,4,3,2,1,0:T(8,128)(2,1)S(1)}, bf16[1,4,16,2,2,2,3]{2,5,6,4,3,1,0:T(2,128)(2,1)S(1)}) conditional(s32[]{:T(128)} %bitcast.53, (s32[16,8]{0,1:T(8,128)}, bf16[1,1,4,16,2,6144]{5,4,3,2,1,0:T(2,128)(2,1)}, s32[1,16]{1,0:T(1,128)}, ...), branch_computations={%region_0.10_spmd, %region_10.11_spmd, %region_11.12_spmd, %region... | conditional | flops 68673144 | bytes 168208768 | solution.py:717
  6.8 0.8 reshape.229
  7.6 0.1 copy.163
  7.7 0.1 copy.164
  7.9 90.8 %branch_2_fun.2 = (bf16[47,4,2,4,2,384]{5,4,3,2,1,0:T(2,128)(2,1)S(1)}, bf16[47,4,2,4,2,384]{5,4,3,2,1,0:T(2,128)(2,1)S(1)}, bf16[47,4,2,4,2,384]{5,4,3,2,1,0:T(...) custom-call(s32[8,128]{1,0:T(8,128)S(1)} %get-tuple-element.72.plan_, ...), custom_call_target="tpu_custom_call" | custom-call | bytes 20971520 | tf_op jit(solution)/shard_map/cond/branch_2_fun/pallas_call | solution.py:457
  98.7 4.7 %branch_2_fun.3 = (bf16[1,4,16,2,2,16,2,384]{7,6,5,4,3,2,1,0:T(2,128)(2,1)}, bf16[4,32,2,2,3]{4,3,2,1,0:T(2,128)(2,1)S(1)}, bf16[1,4,16,2,8,384]{5,4,3,2,1,0:T(8,128)(2,1)S(1)}) custom-call(s32[8,128]{1,0:T(8,128)S(1)} %get-tuple-element.72.plan_ref, bf16[47,4,2,4,2,384]{5,4,3,2,1,0:T(2,128)(2,1)S(1)} %get-tuple-element.78.refs_0_, ...), custom_call_target="tpu_custom_call" | custom-call | tf_op jit(solution)/shard_map/cond/branch_2_fun/pallas_call | solution.py:530
  103.4 0.3 copy.206
  104.2 0.0 copy-start.9
  104.2 0.0 copy-start.11
  104.3 0.6 copy-done.9
  104.8 0.3 copy-done.11
  (3 shorter events, 0.1 us)
Async XLA Ops:
  104.2 0.6 copy-start.9
  104.2 0.9 copy-start.11
